TPU v7x, 32 devices: a whole 2x2x4 slice. The times are simulated.
32 devices in a mesh: phi: 2 (over x), theta: 4 (over y, core), row: 4 (over z).
Axes of the slice: x: 2, y: 2, z: 4, core: 2. Of those that a mesh axis runs over, the one named last changes fastest.
Arguments:
- fields: float32 [8, 12, 1536, 512], P(None, 'row', 'phi', 'theta'), may hold values from -6 to 6
- kept_counts: int32 [512], replicated, may hold values from 1 to 384, as said below
Outputs:
- filtered: float32 [8, 12, 1536, 512], P(None, 'row', 'phi', 'theta')
Inputs may be any that keep to these rules, and one draw needn't show every extreme that they name: `kept_counts`: modes 0 to count - 1 of a cap row are kept; some row reaches 384 in every draw.
All inputs are finite; a program needn't handle non-finite values.
Results may differ from a plain program's by a relative error of at most 0.00007.
Values sent between devices are 32-bit elements; how exact they have to be, the bound alone decides.
A program may use at most 64 MiB of HBM per device.

v0:
```python
import math

import jax
import jax.numpy as jnp
from jax import lax
from jax.sharding import PartitionSpec as P

KMAX = 384


def tables(offset, span_rows, points, mode_count):
    azimuth = offset + jnp.arange(span_rows, dtype=jnp.int32)
    wavenumber = jnp.arange(mode_count, dtype=jnp.int32)
    phase_turns = azimuth[:, None] * wavenumber[None, :] % points
    angles = phase_turns.astype(jnp.float32) * (2.0 * math.pi / points)
    forward = jnp.concatenate([jnp.cos(angles), jnp.sin(angles)], axis=1)
    weight = jnp.where(wavenumber == 0, 1.0, 2.0).astype(jnp.float32) / points
    weight = jnp.concatenate([weight, weight])
    backward = (forward * weight[None, :]).T
    return (forward, backward)


def spectral(lines, row_counts):
    nfields, shells, local_points, rows_here = lines.shape
    n_phi = lax.axis_size("phi")
    points = local_points * n_phi
    highest = lax.Precision.HIGHEST
    groups = nfields * shells
    grouped = lines.reshape(groups, local_points, rows_here)
    line_counts = jnp.broadcast_to(row_counts[None, :], (groups, rows_here)).reshape(-1)
    phi_index = lax.axis_index("phi")
    forward, backward = tables(phi_index * local_points, local_points, points, KMAX)
    share_rows = forward.shape[1] // n_phi
    out = jnp.einsum(
        "pk,gpr->kgr", forward, grouped, precision=highest, preferred_element_type=jnp.float32
    )
    share = lax.psum_scatter(
        out.reshape(share_rows * lax.axis_size("phi"), groups * rows_here),
        "phi",
        scatter_dimension=0,
        tiled=True,
    )
    share_index = phi_index * share_rows + jnp.arange(share_rows, dtype=jnp.int32)
    keep = (share_index % KMAX)[:, None] < line_counts[None, :]
    masked = jnp.where(keep, share, 0.0)
    piece = lax.all_gather(masked, "phi", axis=0, tiled=True)
    stacked = piece.reshape(piece.shape[0], groups, rows_here)
    result = jnp.einsum(
        "kp,kgr->gpr", backward, stacked, precision=highest, preferred_element_type=jnp.float32
    )
    return result.reshape(lines.shape)


def on_device(fields, kept_counts):
    n_theta = lax.axis_size("theta")
    theta_index = lax.axis_index("theta")
    band_rows = fields.shape[3]
    caps = kept_counts.shape[0] // band_rows
    cap_bands = caps // 2
    count_table = kept_counts.reshape(caps, band_rows)
    low_side = theta_index < cap_bands
    high_side = theta_index >= n_theta - cap_bands
    position = jnp.where(low_side, theta_index, theta_index - (n_theta - 2 * cap_bands))
    position = jnp.clip(position, 0, caps - 1)
    row_counts = lax.dynamic_index_in_dim(count_table, position, 0, keepdims=False)
    smoothed = spectral(fields, row_counts)
    return jnp.where(jnp.logical_or(low_side, high_side), smoothed, fields)


def solution(mesh):
    placed = (P(None, "row", "phi", "theta"), P())
    return jax.shard_map(
        on_device,
        mesh=mesh,
        in_specs=placed,
        out_specs=P(None, "row", "phi", "theta"),
        check_vma=False,
    )
```

profile of v0, /device:TPU:0, one launch (start us, length us, event | category | flops | bytes accessed | tf_op | source)
XLA Modules:
  0.0 369.3 jit_solution(2330304398772714068)
XLA Ops:
  6.5 0.0 copy-start
  6.5 0.0 reduce-scatter.2.cloned.1.call-start
  6.5 4.8 %fusion.10 = (f32[768,384]{1,0:T(8,128)S(1)}, f32[768,384]{1,0:T(8,128)S(1)}) fusion(s32[768]{0:T(1024)S(1)} %iota_add_fusion), kind=kLoop, calls=%fused_computation.15 | loop fusion | flops 2654208 | bytes 2362368 | tf_op jit(solution)/shard_map/cos | solution.py:16
  11.4 9.6 %copy.5 = f32[8,3,768,128]{2,3,1,0:T(8,128)} copy(f32[8,3,768,128]{3,2,1,0:T(8,128)} %param.2) | data formatting | bytes 18874368 | tf_op args[0]
  21.0 49.8 %fusion.3 = f32[768,3072]{1,0:T(8,128)} fusion(f32[3072,768]{1,0:T(8,128)} %bitcast.22, f32[768,384]{1,0:T(8,128)S(1)} %get-tuple-element.6, f32[768,384]{1,0:T(8,128)S(1)} %get-tuple-element.5), kind=kOutput, calls=%fused_computation.6 | convolution fusion | flops 21743861760 | bytes 21233664 | tf_op jit(solution)/shard_map/pk,gpr->kgr/dot_general | solution.py:34
  70.8 0.0 reduce-scatter.2.cloned.1.call-update
  70.8 0.0 all-gather.2.cloned.1.call-start
  70.9 0.0 copy-done
  70.9 113.3 %reduce-scatter.2.cloned.1.call-done = f32[384,3072]{1,0:T(8,128)} async-done(((f32[768,3072]{1,0:T(8,128)}), f32[384,3072]{1,0:T(8,128)}) %reduce-scatter.2.cloned.1.call-update) | async-done | bytes 4718608 | tf_op jit(solution)/shard_map/reduce_scatter | solution.py:37
  184.2 5.5 %compare_select_fusion = f32[384,3072]{1,0:T(8,128)} fusion(f32[384,3072]{1,0:T(8,128)} %reduce-scatter.2.cloned.1.call-done, s32[3072]{0:T(1024)S(1)} %broadcast_bitcast_fusion, s32[384]{0:T(512)S(1)} %add_select_fusion.1), kind=kLoop, calls=%fused_computation | loop fusion | flops 2359296 | bytes 9451008 | tf_op jit(solution)/shard_map/jit(_where)/select_n | solution.py:45
  189.7 0.0 all-gather.2.cloned.1.call-update
  189.7 118.1 %all-gather.2.cloned.1.call-done = f32[768,3072]{1,0:T(8,128)} async-done(((f32[384,3072]{1,0:T(8,128)}), f32[768,3072]{1,0:T(8,128)}) %all-gather.2.cloned.1.call-update) | async-done | bytes 9437200 | tf_op jit(solution)/shard_map/all_gather | solution.py:46
  307.9 9.6 %copy.8 = f32[768,3072]{0,1:T(8,128)} copy(f32[768,3072]{1,0:T(8,128)} %all-gather.2.cloned.1.call-done) | data formatting | bytes 18874368 | tf_op jit(solution)/shard_map/reshape | solution.py:47
  317.5 26.8 %fusion = f32[24,128,768]{2,1,0:T(8,128)} fusion(f32[768,24,128]{0,2,1:T(8,128)} %bitcast.20, f32[768,384]{1,0:T(8,128)S(1)} %get-tuple-element.6, f32[768,384]{1,0:T(8,128)S(1)} %get-tuple-element.5, f32[768]{0:T(1024)S(1)} %pad_maximum_fusion.3), kind=kOutput, calls=%fused_computation.3 | convolution fusion | flops 21744451584 | bytes 21236736 | tf_op jit(solution)/shard_map/kp,kgr->gpr/dot_general | solution.py:48
  344.2 9.6 %copy.7 = f32[8,3,768,128]{3,2,1,0:T(8,128)} copy(f32[8,3,768,128]{2,3,1,0:T(8,128)} %bitcast.21) | data formatting | bytes 18874368 | tf_op jit(solution)/shard_map/reshape | solution.py:51
  353.8 0.0 copy-start.1
  353.8 8.7 %broadcast_select_fusion = f32[8,3,768,128]{3,2,1,0:T(8,128)} fusion(f32[8,3,768,128]{3,2,1,0:T(8,128)} %copy.7, f32[8,3,768,128]{3,2,1,0:T(8,128)} %param.2, pred[]{:T(512)S(6)} %or.3), kind=kLoop, calls=%fused_computation.1 | loop fusion | flops 2359296 | bytes 28311552 | tf_op jit(solution)/shard_map/jit(_where)/select_n | solution.py:67
  362.5 0.0 copy-done.1
  (6 shorter events, 0.0 us)
Async XLA Ops:
  6.5 64.3 %copy-start = (s32[512]{0:T(512)S(1)}, s32[512]{0:T(512)}, u32[]{:S(2)}) copy-start(s32[512]{0:T(512)} %param.3) | copy-start | bytes 6148
  6.5 177.7 %reduce-scatter.2.cloned.1.call-start = ((), (), s32[]{:S(2)}) async-start(), calls=%async_computation.1 | async-start | bytes 14155776 | tf_op jit(solution)/shard_map/reduce_scatter | solution.py:37
  70.8 237.0 %all-gather.2.cloned.1.call-start = ((), (), s32[]{:S(2)}) async-start(), calls=%async_computation.2 | async-start | bytes 14155776 | tf_op jit(solution)/shard_map/all_gather | solution.py:46
  353.8 8.7 %copy-start.1 = (s32[512]{0:T(512)S(1)}, s32[512]{0:T(512)}, u32[]{:S(2)}) copy-start(s32[512]{0:T(512)} %param.3) | copy-start | bytes 6148
Sparse Core Ops, SparseCore 0:
  70.9 113.2 reduce-scatter.1
  189.8 118.0 all-gather.1
where the time goes:
time: 370 us; the launch traced here: 369 us
  waiting for transfers between devices  231 us (62%)
  matrix products  76.6 us (21%)
  local copies, waits for them, and re-layouts  28.8 us (8%)
  other arithmetic  19 us (5%)
  between operations  13.5 us (4%)
    all_gather x1, waiting for transfers between devices, spectral(): piece = lax.all_gather(masked, 'phi', axis=0, tiled=True)  118 us
    reduce_scatter x1, waiting for transfers between devices, spectral(): lax.psum_scatter(out.reshape(share_rows * lax.axis_size('phi'), groups *...  113 us
    dot_general x1, matrix products, spectral(): jnp.einsum('pk,gpr->kgr', forward, grouped, precision=highest, preferred_...  49.8 us
    dot_general x1, matrix products, spectral(): jnp.einsum('kp,kgr->gpr', backward, stacked, precision=highest, preferred...  26.8 us
    unnamed x5, local copies, waits for them, and re-layouts  9.62 us
    reshape x1, local copies, waits for them, and re-layouts, spectral(): return result.reshape(lines.shape)  9.58 us
    reshape x1, local copies, waits for them, and re-layouts, spectral(): stacked = piece.reshape(piece.shape[0], groups, rows_here)  9.58 us
    select_n x1, other arithmetic, on_device(): return jnp.where(jnp.logical_or(low_side, high_side), smoothed, fields)  8.68 us
  transfers between devices with their start and end apart: 2, of which 2 were waited for; matrix products, arithmetic and copies ran while one was open for 0% of the time, Pallas kernels for 0%

commit v1 on v0

--- a/solution.py
+++ b/solution.py
@@ -1,11 +1,18 @@
+import functools
 import math
 
 import jax
 import jax.numpy as jnp
+import ml_dtypes
+import numpy as np
 from jax import lax
+from jax.experimental import pallas as pl
+from jax.experimental.pallas import tpu as pltpu
 from jax.sharding import PartitionSpec as P
 
 KMAX = 384
+TILE = 128
+LANES = 128
 
 
 def tables(offset, span_rows, points, mode_count):
@@ -51,6 +58,266 @@
     return result.reshape(lines.shape)
 
 
+def halves(x):
+    high = x.astype(jnp.bfloat16)
+    return high, (x - high.astype(jnp.float32)).astype(jnp.bfloat16)
+
+
+def host_halves(x):
+    x = x.astype(np.float32)
+    high = x.astype(ml_dtypes.bfloat16)
+    return high, (x - high.astype(np.float32)).astype(ml_dtypes.bfloat16)
+
+
+def host_tables(half):
+    points = 2 * half
+    azimuth = np.arange(half)
+    mode = np.arange(KMAX)
+    angle = (mode[:, None] * azimuth[None, :] % points) * (2.0 * math.pi / points)
+    cos, sin = np.cos(angle), np.sin(angle)
+    weight = (np.where(mode == 0, 1.0, 2.0) / points)[:, None]
+    up = np.concatenate([cos, sin])
+    down = np.concatenate([cos[::-1], sin[::-1]])
+    up_back = np.concatenate([cos * weight, sin * weight]).T
+    down_back = np.concatenate([(cos * weight)[::-1], (sin * weight)[::-1]]).T
+    return [part for t in (up, down, up_back, down_back) for part in host_halves(t)]
+
+
+def order_kernel(all_ref, own_ref, spread_ref, gather_ref, kept_ref, longest_ref):
+    half = LANES // 2
+
+    def sort(counts):
+        across = jnp.broadcast_to(counts, (LANES, LANES))
+        down = across.T
+        lane = lax.broadcasted_iota(jnp.int32, (LANES, LANES), 1)
+        line = lax.broadcasted_iota(jnp.int32, (LANES, LANES), 0)
+        ahead = jnp.where((across > down) | ((across == down) & (lane < line)), 1.0, 0.0)
+        behind = jnp.where((down > across) | ((across == down) & (line < lane)), 1.0, 0.0)
+        rank_down = jnp.sum(ahead, axis=1, keepdims=True)
+        rank_across = jnp.sum(behind, axis=0, keepdims=True)
+        place = lambda r: jnp.where(r < half, r, 2.0 * LANES - 1.0 - r)
+        to_down = jnp.concatenate([place(rank_down), place(rank_down) + half], axis=0)
+        to_across = jnp.concatenate([place(rank_across), place(rank_across) + half], axis=1)
+        lane2 = lax.broadcasted_iota(jnp.int32, (2 * LANES, 2 * LANES), 1).astype(jnp.float32)
+        line2 = lax.broadcasted_iota(jnp.int32, (2 * LANES, 2 * LANES), 0).astype(jnp.float32)
+        spread = jnp.where(lane2 == to_down, 1.0, 0.0)
+        gather = jnp.where(line2 == to_across, 1.0, 0.0)
+        counts_down = jnp.concatenate([down[:, :1], down[:, :1]], axis=0)
+        kept = jnp.sum(spread * counts_down, axis=0, keepdims=True)
+        return spread, gather, kept
+
+    spread, gather, kept = sort(own_ref[...].astype(jnp.float32))
+    spread_ref[...] = spread.astype(jnp.bfloat16)
+    gather_ref[...] = gather.astype(jnp.bfloat16)
+    kept_ref[...] = kept.astype(jnp.int32)
+    longest = jnp.zeros((1, LANES), jnp.float32)
+    for band in range(all_ref.shape[0]):
+        _, _, kept = sort(all_ref[band : band + 1, :].astype(jnp.float32))
+        longest = jnp.maximum(longest, kept[:, :LANES] + kept[:, LANES:])
+    longest_ref[0] = jnp.max(longest).astype(jnp.int32)
+
+
+def exchange_kernel(
+    length,
+    x_hbm,
+    *refs,
+):
+    table_hbm = refs[:8]
+    spread_ref, gather_ref, kept_ref, out_hbm = refs[8:12]
+    table = refs[12:20]
+    x_ref, send_ref, recv_ref, sign_ref, large, small, c_large, c_small = refs[20:28]
+    table_sem, in_sem, out_sem, send_sem, recv_sem = refs[28:]
+    steps = x_ref.shape[0]
+    points = x_ref.shape[2]
+    start_small = length - KMAX
+    other = 1 - lax.axis_index("phi")
+
+    def copy_in(s):
+        return pltpu.make_async_copy(x_hbm.at[pl.ds(2 * s, 2)], x_ref.at[s], in_sem.at[s])
+
+    def copy_out(s):
+        return pltpu.make_async_copy(x_ref.at[s], out_hbm.at[pl.ds(2 * s, 2)], out_sem.at[s])
+
+    def copy_table(i):
+        return pltpu.make_async_copy(table_hbm[i], table[i], table_sem.at[i])
+
+    def exchange(s):
+        return pltpu.make_async_remote_copy(
+            src_ref=send_ref.at[s],
+            dst_ref=recv_ref.at[s],
+            send_sem=send_sem.at[s],
+            recv_sem=recv_sem.at[s],
+            device_id={"phi": other},
+            device_id_type=pl.DeviceIdType.MESH,
+        )
+
+    copy_in(0).start()
+    for i in range(4):
+        copy_table(i).start()
+    barrier = pltpu.get_barrier_semaphore()
+    pl.semaphore_signal(
+        barrier, inc=1, device_id={"phi": other}, device_id_type=pl.DeviceIdType.MESH
+    )
+
+    @pl.loop(1, steps)
+    def _(s):
+        copy_in(s).start()
+
+    for i in range(4, 8):
+        copy_table(i).start()
+
+    kept_large = kept_ref[:, :LANES]
+    kept_small = kept_ref[:, LANES:]
+    row = lax.broadcasted_iota(jnp.int32, (length, LANES), 0)
+    parity = jnp.where(row < kept_large, row, length - 1 - row) % 2
+    sign_ref[...] = 1.0 - 2.0 * parity.astype(jnp.float32)
+    mode = lax.broadcasted_iota(jnp.int32, (KMAX, LANES), 0)
+
+    def dot(a, b):
+        return jnp.dot(a, b, preferred_element_type=jnp.float32)
+
+    def product(high_ref, low_ref, rows, operand):
+        wide = dot(high_ref[rows, :], operand[...])
+        return wide[:, :LANES] + wide[:, LANES:] + dot(low_ref[rows, :], operand[:, :LANES])
+
+    for i in range(4):
+        copy_table(i).wait()
+    pl.semaphore_wait(barrier, 1)
+
+    @pl.loop(0, steps)
+    def _(s):
+        copy_in(s).wait()
+
+        @pl.loop(0, points // TILE)
+        def _(t):
+            rows = pl.ds(pl.multiple_of(t * TILE, TILE), TILE)
+            both = jnp.concatenate([x_ref[s, 0, rows, :], x_ref[s, 1, rows, :]], axis=1)
+            high, low = halves(both)
+            high = dot(high, spread_ref[...]).astype(jnp.bfloat16)
+            low = dot(low, spread_ref[...]).astype(jnp.bfloat16)
+            large[rows, :] = jnp.concatenate([high[:, :LANES], low[:, :LANES]], axis=1)
+            small[rows, :] = jnp.concatenate([high[:, LANES:], low[:, LANES:]], axis=1)
+
+        @pl.loop(0, 2 * KMAX // TILE)
+        def _(t):
+            rows = pl.ds(pl.multiple_of(t * TILE, TILE), TILE)
+            c_large[rows, :] = product(table[0], table[1], rows, large)
+            c_small[rows, :] = product(table[2], table[3], rows, small)
+
+        for part in range(2):
+            rows = pl.ds(part * KMAX, KMAX)
+            down = jnp.where(KMAX - 1 - mode < kept_small, c_small[rows, :], 0.0)
+            up = jnp.where(mode < kept_large, c_large[rows, :], 0.0)
+            send_ref[s, part, pl.ds(0, KMAX), :] = up
+            if start_small < KMAX:
+                shared = KMAX - start_small
+                send_ref[s, part, pl.ds(start_small, shared), :] = up[start_small:] + down[:shared]
+            if start_small > 0:
+                send_ref[s, part, pl.ds(KMAX, start_small), :] = down[KMAX - start_small :]
+        exchange(s).start()
+
+    for i in range(4, 8):
+        copy_table(i).wait()
+
+    @pl.loop(0, steps)
+    def _(s):
+        exchange(s).wait_recv()
+        for part in range(2):
+            rows = pl.ds(part * KMAX, KMAX)
+            total = send_ref[s, part] + sign_ref[...] * recv_ref[s, part]
+            up = jnp.where(mode < kept_large, total[:KMAX], 0.0)
+            down = jnp.where(KMAX - 1 - mode < kept_small, total[start_small:], 0.0)
+            large[rows, :] = jnp.concatenate(halves(up), axis=1)
+            small[rows, :] = jnp.concatenate(halves(down), axis=1)
+
+        @pl.loop(0, points // TILE)
+        def _(t):
+            rows = pl.ds(pl.multiple_of(t * TILE, TILE), TILE)
+            result = jnp.concatenate(
+                [
+                    product(table[4], table[5], rows, large),
+                    product(table[6], table[7], rows, small),
+                ],
+                axis=1,
+            )
+            high, low = halves(result)
+            result = dot(high, gather_ref[...]) + dot(low, gather_ref[...])
+            x_ref[s, 0, rows, :] = result[:, :LANES]
+            x_ref[s, 1, rows, :] = result[:, LANES:]
+
+        copy_out(s).start()
+
+    @pl.loop(0, steps)
+    def _(s):
+        exchange(s).wait_send()
+        copy_out(s).wait()
+
+
+def exchange(length, collective_id, lines, host, spread, gather, kept):
+    groups, points, lanes = lines.shape
+    steps = groups // 2
+    anywhere = pl.BlockSpec(memory_space=pl.ANY)
+    inside = pl.BlockSpec(memory_space=pltpu.VMEM)
+    dma = pltpu.SemaphoreType.DMA
+    deep = max(points, 2 * KMAX)
+    return pl.pallas_call(
+        functools.partial(exchange_kernel, length),
+        out_shape=jax.ShapeDtypeStruct(lines.shape, jnp.float32),
+        in_specs=[anywhere] * 9 + [inside] * 3,
+        out_specs=anywhere,
+        scratch_shapes=[pltpu.VMEM(t.shape, jnp.bfloat16) for t in host]
+        + [
+            pltpu.VMEM((steps, 2, points, lanes), jnp.float32),
+            pltpu.VMEM((steps, 2, length, lanes), jnp.float32),
+            pltpu.VMEM((steps, 2, length, lanes), jnp.float32),
+            pltpu.VMEM((length, lanes), jnp.float32),
+            pltpu.VMEM((deep, 2 * lanes), jnp.bfloat16),
+            pltpu.VMEM((deep, 2 * lanes), jnp.bfloat16),
+            pltpu.VMEM((2 * KMAX, lanes), jnp.float32),
+            pltpu.VMEM((2 * KMAX, lanes), jnp.float32),
+            dma((8,)),
+            dma((steps,)),
+            dma((steps,)),
+            dma((steps,)),
+            dma((steps,)),
+        ],
+        compiler_params=pltpu.CompilerParams(
+            collective_id=collective_id,
+            has_side_effects=True,
+            vmem_limit_bytes=56 * 1024 * 1024,
+        ),
+        name="exchange_" + str(length),
+    )(lines, *host, spread, gather, kept)
+
+
+LENGTHS = (400, 416, 432, 448, 480, 576, 2 * KMAX)
+
+
+def paired(lines, count_table, row_counts):
+    nfields, shells, points, lanes = lines.shape
+    whole = pl.BlockSpec(memory_space=pltpu.VMEM)
+    spread, gather, kept, longest = pl.pallas_call(
+        order_kernel,
+        out_shape=(
+            jax.ShapeDtypeStruct((2 * lanes, 2 * lanes), jnp.bfloat16),
+            jax.ShapeDtypeStruct((2 * lanes, 2 * lanes), jnp.bfloat16),
+            jax.ShapeDtypeStruct((1, 2 * lanes), jnp.int32),
+            jax.ShapeDtypeStruct((1,), jnp.int32),
+        ),
+        in_specs=[whole, whole],
+        out_specs=(whole, whole, whole, pl.BlockSpec(memory_space=pltpu.SMEM)),
+        name="order_rows",
+    )(count_table, row_counts[None, :])
+    host = [jnp.asarray(t) for t in host_tables(points)]
+    branch = jnp.sum((longest[0] > jnp.asarray(LENGTHS[:-1], jnp.int32)).astype(jnp.int32))
+    branches = [
+        functools.partial(exchange, length, index) for index, length in enumerate(LENGTHS)
+    ]
+    grouped = lines.reshape(nfields * shells, points, lanes)
+    result = lax.switch(branch, branches, grouped, host, spread, gather, kept)
+    return result.reshape(lines.shape)
+
+
 def on_device(fields, kept_counts):
     n_theta = lax.axis_size("theta")
     theta_index = lax.axis_index("theta")
@@ -63,7 +330,18 @@
     position = jnp.where(low_side, theta_index, theta_index - (n_theta - 2 * cap_bands))
     position = jnp.clip(position, 0, caps - 1)
     row_counts = lax.dynamic_index_in_dim(count_table, position, 0, keepdims=False)
-    smoothed = spectral(fields, row_counts)
+    fits = (
+        lax.axis_size("phi") == 2
+        and band_rows == LANES
+        and fields.shape[0] * fields.shape[1] % 2 == 0
+        and fields.shape[2] % TILE == 0
+    )
+    if fits:
+        smoothed = paired(fields, count_table, row_counts)
+    else:
+        smoothed = spectral(fields, row_counts)
+    if n_theta == caps:
+        return smoothed
     return jnp.where(jnp.logical_or(low_side, high_side), smoothed, fields)
 
 

time: 370 us -> 140 us (0.38)
  waiting for transfers between devices: 231 us -> 0 us
  Pallas kernels: 0 us -> 130 us
  matrix products: 76.6 us -> 0 us
  local copies, waits for them, and re-layouts: 28.8 us -> 9.53 us
  other arithmetic: 19 us -> 1.98 us
  between operations: 13.5 us -> 0.67 us
    pallas_call x0 -> x2, Pallas kernels: none -> 130 us  [the longest x1 128 us: exchange(): pl.pallas_call(functools.partial(exchange_kernel, length), out_shape=jax....]
    all_gather x1 -> x0, waiting for transfers between devices: 118 us -> none  [spectral(): piece = lax.all_gather(masked, 'phi', axis=0, tiled=True)]
    reduce_scatter x1 -> x0, waiting for transfers between devices: 113 us -> none  [spectral(): lax.psum_scatter(out.reshape(share_rows * lax.axis_size('phi'), groups *...]
    dot_general x2 -> x0, matrix products: 76.6 us -> none  [the longest x1 49.8 us: spectral(): jnp.einsum('pk,gpr->kgr', forward, grouped, precision=highest, preferred_...]
    reshape x2 -> x0, local copies, waits for them, and re-layouts: 19.2 us -> none  [the longest x1 9.58 us: spectral(): return result.reshape(lines.shape)]
    select_n x3 -> x0, other arithmetic: 14.2 us -> none  [the longest x1 8.68 us: on_device(): return jnp.where(jnp.logical_or(low_side, high_side), smoothed, fields)]
    cos x1 -> x0, other arithmetic: 4.83 us -> none  [tables(): forward = jnp.concatenate([jnp.cos(angles), jnp.sin(angles)], axis=1)]
    unnamed x5 -> x1, local copies, waits for them, and re-layouts: 9.62 us -> 8.33 us
  transfers between devices with their start and end apart: 2 -> 0, of which waited for: 2 -> 0; matrix products, arithmetic and copies ran while one was open for 0% -> 0% of each run, Pallas kernels for 0% -> 0%
where the time goes in v1:
time: 140 us; the launch traced here: 142 us
  Pallas kernels  130 us (93%)
  local copies, waits for them, and re-layouts  9.53 us (7%)
  other arithmetic  1.98 us (1%)
    pallas_call x1, Pallas kernels, exchange(): pl.pallas_call(functools.partial(exchange_kernel, length), out_shape=jax....  128 us
    unnamed x1, local copies, waits for them, and re-layouts  8.33 us

profile of v1, /device:TPU:0, one launch (start us, length us, event | category | flops | bytes accessed | tf_op | source)
XLA Modules:
  0.0 142.2 jit_solution(3977850614574842250)
XLA Ops:
  0.0 1.2 constant_dynamic-slice_fusion.own_ref
  1.2 1.9 %order_rows.1 = (bf16[256,256]{1,0:T(8,128)(2,1)S(1)}, bf16[256,256]{1,0:T(8,128)(2,1)S(1)}, s32[1,256]{1,0:T(1,128)S(1)}, s32[1]{0:T(128)}) custom-call(s32[4,128]{1,0:T(4,128)} %bitcast.25, s32[1,128]{1,0:T(1,128)} %constant_dynamic-slice_fusion.own_ref), custom_call_target="tpu_custom_call" | custom-call | tf_op jit(solution)/shard_map/order_rows/pallas_call | solution.py:299
  3.1 2.0 %fusion = s32[]{:T(128)} fusion(s32[6]{0:T(128)} %constant.43.clone, s32[]{:T(128)} %bitcast.8), kind=kLoop, calls=%fused_computation.1 | loop fusion | flops 17 | bytes 32 | tf_op jit(solution)/shard_map/reduce_sum | solution.py:312
  5.8 128.1 %conditional.1 = (f32[8,3,768,128]{3,2,1,0:T(8,128)}) conditional(s32[]{:T(128)} %clamp.3, (f32[24,768,128]{2,1,0:T(8,128)}, bf16[768,768]{1,0:T(8,128)(2,1)}, bf16[768,768]{1,0:T(8,128)(2,1)}, bf16[768,768]{1,0:T(8,128)(2,1)}, bf16[768,768]{1,0:T(8,128)(2,1)}, /*index=5*/bf16[768,768]{1,0:T(8,128)(2,1)}, ...), branch_computations={%region_1.2_spmd, %region_2.3_spmd, %region_3.4_spmd, %region_4.5_... | conditional | bytes 8 | solution.py:317
  5.8 128.1 %exchange_432.1 = f32[24,768,128]{2,1,0:T(8,128)} custom-call(f32[24,768,128]{2,1,0:T(8,128)} %get-tuple-element.206.x_hbm, bf16[768,768]{1,0:T(8,128)(2,1)} %get-tuple-element.207.refs_0_, bf16[768,768]{1,0:T(8,128)(2,1)} %get-tuple-element.208.refs_1_, bf16[768,768]{1,0:T(8,128)(2,1)} %get-tuple-element.209.refs_2_, ...), custom_call_target="tpu_custom_call" | custom-call | tf_op jit(solution)/shard_map/cond/branch_2_fun/exchange_432/pallas_call | solution.py:263
  133.9 8.3 %copy.27 = f32[8,3,768,128]{3,2,1,0:T(8,128)} copy(f32[8,3,768,128]{3,2,1,0:T(8,128)} %get-tuple-element.274) | data formatting | bytes 18874368
